TPU v7x, 32 devices: a whole 2x2x4 slice. The times are simulated.
32 devices in a mesh: groups: 2 (over x), row: 8 (over z, y), col: 2 (over core).
Axes of the slice: x: 2, y: 2, z: 4, core: 2. Of those that a mesh axis runs over, the one named last changes fastest.
Arguments:
- positions: float32 [32768, 384], P(('groups', 'row', 'col')), parts along dimension 0, may hold values from -1 to 1
- momenta: float32 [32768, 384], P(('groups', 'row', 'col')), parts along dimension 0, may hold values from -3 to 3
- tile_values: bfloat16 [3072, 128, 128], P(('groups', 'row', 'col')), parts along dimension 0, may hold values from -0.19921875 to 0.19921875
- tile_rows: int32 [3072], P(('groups', 'row', 'col')), parts along dimension 0, may hold values from 0 to 7
- tile_cols: int32 [3072], P(('groups', 'row', 'col')), parts along dimension 0, may hold values from 0 to 23
- tile_count: int32 [32], P(('groups', 'row', 'col')), parts along dimension 0, may hold values from 24 to 96, as said below
- channel_coupling: bfloat16 [48, 48], replicated, may hold values from -0.875 to 0.875
Outputs:
- new_positions: float32 [32768, 384], P(('groups', 'row', 'col')), parts along dimension 0
- new_momenta: float32 [32768, 384], P(('groups', 'row', 'col')), parts along dimension 0
- energy: float32 [16], P('groups'), parts along dimension 0
There are 2 independent parts, one for each index of `groups`. A program takes and returns all parts, laid end to end along the dimension named above; an argument that names none is the same for every part. Nothing has to cross between parts.
Inputs may be any that keep to these rules, and one draw needn't show every extreme that they name: tile_count[b] is the number of live slots of block b; slots at or past it are ignored; some block has exactly 96 live slots.
All inputs are finite; a program needn't handle non-finite values.
Results may differ from a plain program's by a relative error of at most 0.00079.
Values may be sent and summed in bfloat16 or wider, within the bound.
No kernel may reach another device: no remote copies, remote signals or barrier semaphores. Data moves between devices by JAX's collectives and lax.ppermute only.
A program may use at most 64 MiB of HBM per device.

v0:
```python
import functools

import jax
import jax.numpy as jnp
from jax import lax
from jax.experimental import pallas as pl
from jax.experimental.pallas import tpu as pltpu
from jax.sharding import PartitionSpec as P

STEPS = 2
LANES = 128
UNROLL = 16
VMEM_LIMIT = 40 * 1024 * 1024

SMEM_SPEC = pl.BlockSpec(memory_space=pltpu.SMEM)
VMEM_SPEC = pl.BlockSpec(memory_space=pltpu.VMEM)
ANY_SPEC = pl.BlockSpec(memory_space=pl.ANY)


def params():
    return pltpu.CompilerParams(vmem_limit_bytes=VMEM_LIMIT)


def cost(flops, moved):
    return pl.CostEstimate(flops=int(flops), bytes_accessed=int(moved), transcendentals=0)


def lanes(group):
    return slice(group * LANES, (group + 1) * LANES)


def spanned(group, channels, width):
    first = group * LANES // channels * channels
    last = -(-(group + 1) * LANES // channels) * channels
    return list(range(first // LANES, -(-min(last, width) // LANES)))


def round_group(positions, group):
    cells = positions.shape[0]

    def body(x_ref, out_ref):
        out_ref[...] = x_ref[...].astype(jnp.bfloat16)

    return pl.pallas_call(
        body,
        grid=(1,),
        in_specs=[pl.BlockSpec((cells, LANES), lambda i: (0, group))],
        out_specs=pl.BlockSpec((cells, LANES), lambda i: (0, 0)),
        out_shape=jax.ShapeDtypeStruct((cells, LANES), jnp.bfloat16),
        compiler_params=params(),
        cost_estimate=cost(0, cells * LANES * 6),
        name="round_group",
    )(positions)


def base_values(xs, ys, same, step, channels):
    groups = len(xs)
    cells = xs[0].shape[0]
    width = groups * LANES
    detune = 1.0 - (step + 1.0) / (STEPS + 1.0)

    def body(*refs):
        x_refs, y_refs = refs[:groups], refs[groups : 2 * groups]
        same_ref, out_refs = refs[2 * groups], refs[2 * groups + 1 :]
        high = [r[...].astype(jnp.bfloat16) for r in x_refs]
        low = [
            (r[...] - h.astype(jnp.float32)).astype(jnp.bfloat16) for r, h in zip(x_refs, high)
        ]
        for g in range(groups):
            near = spanned(g, channels, width)
            part = slice(near[0] * LANES, (near[-1] + 1) * LANES)
            ones = same_ref[part, lanes(g)]
            totals = jnp.dot(
                jnp.concatenate([high[n] for n in near], axis=1),
                ones,
                preferred_element_type=jnp.float32,
            ) + jnp.dot(
                jnp.concatenate([low[n] for n in near], axis=1),
                ones,
                preferred_element_type=jnp.float32,
            )
            penalty = 0.02 * (totals - (2.0 - channels))
            out_refs[g][...] = y_refs[g][...] + 0.5 * (
                -detune * x_refs[g][...] - 0.4 * penalty
            )

    return pl.pallas_call(
        body,
        in_specs=[VMEM_SPEC] * (2 * groups + 1),
        out_specs=[VMEM_SPEC] * groups,
        out_shape=[jax.ShapeDtypeStruct((cells, LANES), jnp.float32)] * groups,
        compiler_params=params(),
        cost_estimate=cost(4 * cells * width * width, cells * width * 12),
        name="base_values",
    )(*xs, *ys, same)


def field_into(rows, cols, count, tiles, parts, field, window):
    slots, tile, _ = tiles.shape
    spare = field.shape[0] - 1
    per = window.shape[0] // len(parts)
    for k, part in enumerate(parts):
        window[k * per : (k + 1) * per] = part[...].reshape(per, tile, LANES)
    field[...] = jnp.zeros_like(field)
    live = count[0]

    def some(start, unroll):
        for u in range(unroll):
            slot = start + u
            row = jnp.where(slot < live, rows[slot], spare)
            field[row] += jnp.dot(
                tiles[slot], window[cols[slot]], preferred_element_type=jnp.float32
            )

    whole = slots // UNROLL

    def body(i, carry):
        some(i * UNROLL, UNROLL)
        return carry

    lax.fori_loop(0, whole, body, 0)
    some(whole * UNROLL, slots - whole * UNROLL)


def stage(
    slot_args,
    parts,
    others,
    updates,
    mixing,
    channels,
    field_group,
    final,
):
    rows, cols, count, tiles = slot_args
    slots, tile, _ = tiles.shape
    cells = parts[0].shape[0]
    width = mixing.shape[0]
    keys = sorted(others)
    per = cells // tile

    def body(*refs):
        refs = list(refs)
        rows_ref, cols_ref, count_ref, tiles_ref = refs[:4]
        part_refs = refs[4:7]
        refs = refs[7:]
        other_refs = dict(zip(keys, refs[: len(keys)]))
        refs = refs[len(keys) :]
        mixing_ref, refs = refs[0], refs[1:]
        update_refs = [refs[i * 3 : i * 3 + 3] for i in range(len(updates))]
        refs = refs[3 * len(updates) :]
        out_refs, (field, window) = refs[:-2], refs[-2:]
        field_into(rows_ref, cols_ref, count_ref, tiles_ref, part_refs, field, window)
        own = field[:per].reshape(cells, LANES).astype(jnp.bfloat16)
        out_refs[0][...] = own
        out_refs = out_refs[1:]
        for i, (group, *_) in enumerate(updates):
            base_ref, x_ref, rounded_ref = update_refs[i]
            x_out, y_out, last_out = out_refs[3 * i : 3 * i + 3]
            near = spanned(group, channels, width)
            part = slice(near[0] * LANES, (near[-1] + 1) * LANES)
            mixed = jnp.dot(
                jnp.concatenate(
                    [own if n == field_group else other_refs[n][...] for n in near], axis=1
                ),
                mixing_ref[part, lanes(group)],
                preferred_element_type=jnp.float32,
            )
            y_new = base_ref[...] - 0.2 * mixed
            x_new = jnp.clip(x_ref[...] + 0.5 * y_new, -1.0, 1.0)
            y_out[...] = y_new
            x_out[...] = x_new
            if final:
                weighted = rounded_ref[...].astype(jnp.float32) * mixed
                last_out[...] = jnp.sum(weighted, axis=0, keepdims=True)
            else:
                last_out[...] = x_new.astype(jnp.bfloat16)

    f32 = jax.ShapeDtypeStruct((cells, LANES), jnp.float32)
    b16 = jax.ShapeDtypeStruct((cells, LANES), jnp.bfloat16)
    lane = jax.ShapeDtypeStruct((1, LANES), jnp.float32)
    shapes = [b16]
    for _ in updates:
        shapes += [f32, f32, lane if final else b16]
    flat = [a for _, *arrays in updates for a in arrays]
    outs = pl.pallas_call(
        body,
        in_specs=[SMEM_SPEC] * 3 + [VMEM_SPEC] * (5 + len(keys) + len(flat)),
        out_specs=[VMEM_SPEC] * len(shapes),
        out_shape=shapes,
        scratch_shapes=[
            pltpu.VMEM((per + 1, tile, LANES), jnp.float32),
            pltpu.VMEM((3 * per, tile, LANES), jnp.bfloat16),
        ],
        compiler_params=params(),
        cost_estimate=cost(8 * slots * tile * tile * LANES, slots * tile * tile * 2),
        name="stage",
    )(rows, cols, count, tiles, *parts, *[others[k] for k in keys], mixing, *flat)
    return outs[0], [outs[1 + 3 * i : 4 + 3 * i] for i in range(len(updates))]


def local(positions, momenta, tile_values, tile_rows, tile_cols, tile_count, channel_coupling):
    cells, width = positions.shape
    channels = channel_coupling.shape[0]
    replicas = width // channels
    groups = width // LANES
    ring = lax.axis_size("row") * lax.axis_size("col")
    eye = jnp.eye(replicas, dtype=jnp.bfloat16)
    mixing = (eye[:, None, :, None] * channel_coupling[None, :, None, :]).reshape(width, width)
    same = jnp.repeat(jnp.repeat(eye, channels, axis=0), channels, axis=1)
    slot_args = (tile_rows, tile_cols, tile_count, tile_values)
    ahead = [(i, (i + 1) % ring) for i in range(ring)]
    back = [((i + 1) % ring, i) for i in range(ring)]

    def exchange(mine):
        return [
            lax.ppermute(mine, ("row", "col"), ahead),
            mine,
            lax.ppermute(mine, ("row", "col"), back),
        ]

    ready = {g: [] for g in range(groups)}
    for g in range(groups):
        ready[max(spanned(g, channels, width))].append(g)

    xs = [positions[:, lanes(g)] for g in range(groups)]
    ys = [momenta[:, lanes(g)] for g in range(groups)]
    rounded = [round_group(positions, g) for g in range(groups)]
    energies = [None] * groups
    for step in range(STEPS):
        final = step == STEPS - 1
        windows = [exchange(r) for r in rounded]
        bases = base_values(xs, ys, same, step, channels)
        interference = {}
        new_x, new_y, new_r = [None] * groups, [None] * groups, [None] * groups
        for g in range(groups):
            todo = ready[g]
            needed = {n for t in todo for n in spanned(t, channels, width)} - {g}
            interference[g], done = stage(
                slot_args,
                windows[g],
                {n: interference[n] for n in needed},
                [(t, bases[t], xs[t], rounded[t]) for t in todo],
                mixing,
                channels,
                g,
                final,
            )
            for t, (x, y, r) in zip(todo, done):
                new_x[t], new_y[t], new_r[t] = x, y, r
        xs, ys = new_x, new_y
        if final:
            energies = new_r
        else:
            rounded = new_r
    partial = jnp.concatenate(energies, axis=1).reshape(replicas, channels).sum(axis=1)
    size = 1
    while size < ring:
        partial = partial + lax.ppermute(
            partial, ("row", "col"), [(i, i ^ size) for i in range(ring)]
        )
        size *= 2
    energy = partial / jnp.sqrt(jnp.float32(cells * ring * channels))
    return (jnp.concatenate(xs, axis=1), jnp.concatenate(ys, axis=1), energy)


def solution(mesh):
    cells = P(("groups", "row", "col"), None)
    slots = P(("groups", "row", "col"))
    return jax.shard_map(
        local,
        mesh=mesh,
        in_specs=(cells, cells, P(("groups", "row", "col"), None, None), slots, slots, slots, P()),
        out_specs=(cells, cells, P("groups")),
        check_vma=False,
    )
```

profile of v0, /device:TPU:0, one launch (start us, length us, event | category | flops | bytes accessed | tf_op | source)
XLA Modules:
  0.0 78.0 jit_solution(2304774785948959635)
XLA Ops:
  0.6 1.4 %copy-done = f32[1024,384]{1,0:T(8,128)S(1)} copy-done((f32[1024,384]{1,0:T(8,128)S(1)}, f32[1024,384]{1,0:T(8,128)}, u32[]{:S(2)}) %copy-start) | copy-done | bytes 1572888
  2.0 0.7 round_group.5.refs_5_.refs_12_
  2.8 5.4 %collective-permute-start.5 = (bf16[1024,128]{1,0:T(8,128)(2,1)}, bf16[1024,128]{1,0:T(8,128)(2,1)}, u32[]{:S(2)}, u32[]{:S(2)}) collective-permute-start(bf16[1024,128]{1,0:T(8,128)(2,1)} %round_group.5.refs_5_.refs_12_), channel_id=1, source_target_pairs={{1,0},{2,1},{3,2},{4,3},{5,4},{6,5},{7,6},{8,7},{9,8},{10,9},{11,1... | collective-permute-start | bytes 786440 | tf_op jit(solution)/shard_map/ppermute | solution.py:219
  8.2 0.7 round_group.4.refs_5_.refs_11_
  8.9 4.4 %collective-permute-start.3 = (bf16[1024,128]{1,0:T(8,128)(2,1)}, bf16[1024,128]{1,0:T(8,128)(2,1)}, u32[]{:S(2)}, u32[]{:S(2)}) collective-permute-start(bf16[1024,128]{1,0:T(8,128)(2,1)} %round_group.4.refs_5_.refs_11_), channel_id=1, source_target_pairs={{1,0},{2,1},{3,2},{4,3},{5,4},{6,5},{7,6},{8,7},{9,8},{10,9},{11,1... | collective-permute-start | bytes 786440 | tf_op jit(solution)/shard_map/ppermute | solution.py:219
  13.4 4.5 %collective-permute-start.1 = (bf16[1024,128]{1,0:T(8,128)(2,1)S(1)}, bf16[1024,128]{1,0:T(8,128)(2,1)}, u32[]{:S(2)}, u32[]{:S(2)}) collective-permute-start(bf16[1024,128]{1,0:T(8,128)(2,1)S(1)} %round_group.3.refs_5_.refs_15_), channel_id=1, source_target_pairs={{1,0},{2,1},{3,2},{4,3},{5,4},{6,5},{7,6},{8,7},{9,8},{10,9},{11,1... | collective-permute-start | bytes 786440 | tf_op jit(solution)/shard_map/ppermute | solution.py:219
  18.0 1.3 %copy-done.5 = f32[1024,384]{1,0:T(8,128)S(1)} copy-done((f32[1024,384]{1,0:T(8,128)S(1)}, f32[1024,384]{1,0:T(8,128)}, u32[]{:S(2)}) %copy-start.5) | copy-done | bytes 1572888
  19.3 0.9 %fusion.1 = (f32[1024,128]{1,0:T(8,128)S(1)}, f32[1024,128]{1,0:T(8,128)S(1)}, f32[1024,128]{1,0:T(8,128)}) fusion(f32[1024,384]{1,0:T(8,128)S(1)} %copy-done.5), kind=kLoop, calls=%fused_computation.7 | loop fusion | bytes 3145728 | tf_op jit(solution)/shard_map/slice | solution.py:227
  20.2 1.0 %broadcast_multiply_fusion = bf16[8,48,8,48]{3,2,1,0:T(8,128)(2,1)} fusion(bf16[48,48]{1,0:T(8,128)(2,1)S(1)} %copy-done.6, bf16[8,8]{1,0:T(8,128)(2,1)S(1)} %fusion), kind=kLoop, calls=%fused_computation.2 | loop fusion | flops 147456 | bytes 299648 | tf_op jit(solution)/shard_map/mul | solution.py:209
  22.2 0.2 copy.11.refs_6_
  22.4 1.8 %mul.20.refs_7_.refs_8_.refs_9_ = bf16[384,384]{1,0:T(8,128)(2,1)S(1)} reshape(bf16[8,48,8,48]{3,2,1,0:T(8,128)(2,1)} %broadcast_multiply_fusion) | data formatting | bytes 589824 | tf_op jit(solution)/shard_map/mul | solution.py:209
  24.2 1.0 %copy-done.2 = f32[1024,128]{1,0:T(8,128)S(1)} copy-done((f32[1024,128]{1,0:T(8,128)S(1)}, f32[1024,128]{1,0:T(8,128)}, u32[]{:S(2)}) %copy-start.2) | copy-done | bytes 524312
  25.3 1.2 %base_values.2 = (f32[1024,128]{1,0:T(8,128)S(1)}, f32[1024,128]{1,0:T(8,128)S(1)}, f32[1024,128]{1,0:T(8,128)S(1)}) custom-call(f32[1024,128]{1,0:T(8,128)S(1)} %get-tuple-element.59.refs_0_.refs_10_, f32[1024,128]{1,0:T(8,128)S(1)} %get-tuple-element.60.refs_1_.refs_11_, f32[1024,128]{1,0:T(8,128)S(1)} %get-tuple-element.58.refs_2_.refs_14_, ...), custom_call_target="tpu_custom_call" | custom-call | flops 603979776 | bytes 4718592 | tf_op jit(solution)/shard_map/base_values/pallas_call | solution.py:87
  26.5 0.6 copy-done.1
  27.2 3.1 %stage.6.refs_7_ = bf16[1024,128]{1,0:T(8,128)(2,1)S(1)} custom-call(s32[96]{0:T(128)S(1)} %copy-done.3, s32[96]{0:T(128)S(1)} %copy-done.4, s32[1]{0:T(128)S(6)} %copy.13.refs_2_, bf16[96,128,128]{2,1,0:T(8,128)(2,1)S(1)} %copy-done.1, bf16[1024,128]{1,0:T(8,128)(2,1)} %collective-permute-done.2.refs_4_, bf16[1024,128]{1,0:T(8,128)(2,1)} %round_group.4.refs_5_.refs_11_, ...), custom_call_target="tpu_custom_call" | custom-call | flops 1610612736 | bytes 3145728 | tf_op jit(solution)/shard_map/stage/pallas_call | solution.py:186
  30.3 3.4 %stage.7 = (bf16[1024,128]{1,0:T(8,128)(2,1)S(1)}, f32[1024,128]{1,0:T(8,128)S(1)}, f32[1024,128]{1,0:T(8,128)S(1)}, bf16[1024,128]{1,0:T(8,128)(2,1)S(1)}) custom-call(s32[96]{0:T(128)S(1)} %copy-done.3, s32[96]{0:T(128)S(1)} %copy-done.4, s32[1]{0:T(128)S(6)} %copy.13.refs_2_, bf16[96,128,128]{2,1,0:T(8,128)(2,1)S(1)} %copy-done.1, ...), custom_call_target="tpu_custom_call" | custom-call | flops 1610612736 | bytes 3145728 | tf_op jit(solution)/shard_map/stage/pallas_call | solution.py:186
  33.7 3.8 %collective-permute-start.9 = (bf16[1024,128]{1,0:T(8,128)(2,1)S(1)}, bf16[1024,128]{1,0:T(8,128)(2,1)S(1)}, u32[]{:S(2)}, u32[]{:S(2)}) collective-permute-start(bf16[1024,128]{1,0:T(8,128)(2,1)S(1)} %get-tuple-element.34.refs_5_.refs_11_), channel_id=1, source_target_pairs={{1,0},{2,1},{3,2},{4,3},{5,4},{6,5},{7,6},{8,7},{9,8},{10,9},{11,1... | collective-permute-start | bytes 786440 | tf_op jit(solution)/shard_map/ppermute | solution.py:219
  37.5 3.8 %stage.8 = (bf16[1024,128]{1,0:T(8,128)(2,1)}, f32[1024,128]{1,0:T(8,128)S(1)}, f32[1024,128]{1,0:T(8,128)S(1)}, bf16[1024,128]{1,0:T(8,128)(2,1)S(1)}, f32[1024...) custom-call(s32[96]{0:T(128)S(1)} %copy-done.3, s32[96]{0:T(128)S(1)} %copy-done.4, ...), custom_call_target="tpu_custom_call" | custom-call | flops 1610612736 | bytes 3145728 | tf_op jit(solution)/shard_map/stage/pallas_call | solution.py:186
  41.4 4.4 %collective-permute-start.7 = (bf16[1024,128]{1,0:T(8,128)(2,1)S(1)}, bf16[1024,128]{1,0:T(8,128)(2,1)S(1)}, u32[]{:S(2)}, u32[]{:S(2)}) collective-permute-start(bf16[1024,128]{1,0:T(8,128)(2,1)S(1)} %get-tuple-element.33.refs_5_.refs_12_), channel_id=1, source_target_pairs={{1,0},{2,1},{3,2},{4,3},{5,4},{6,5},{7,6},{8,7},{9,8},{10,9},{11,1... | collective-permute-start | bytes 786440 | tf_op jit(solution)/shard_map/ppermute | solution.py:219
  45.8 4.4 %collective-permute-start.11 = (bf16[1024,128]{1,0:T(8,128)(2,1)S(1)}, bf16[1024,128]{1,0:T(8,128)(2,1)S(1)}, u32[]{:S(2)}, u32[]{:S(2)}) collective-permute-start(bf16[1024,128]{1,0:T(8,128)(2,1)S(1)} %get-tuple-element.43.refs_5_.refs_15_), channel_id=1, source_target_pairs={{1,0},{2,1},{3,2},{4,3},{5,4},{6,5},{7,6},{8,7},{9,8},{10,9},{11,1... | collective-permute-start | bytes 786440 | tf_op jit(solution)/shard_map/ppermute | solution.py:219
  50.3 1.2 %base_values.3 = (f32[1024,128]{1,0:T(8,128)S(1)}, f32[1024,128]{1,0:T(8,128)S(1)}, f32[1024,128]{1,0:T(8,128)S(1)}) custom-call(f32[1024,128]{1,0:T(8,128)S(1)} %get-tuple-element.35.refs_0_.refs_10_, f32[1024,128]{1,0:T(8,128)S(1)} %get-tuple-element.36.refs_1_.refs_11_, f32[1024,128]{1,0:T(8,128)S(1)} %get-tuple-element.37.refs_2_.refs_14_, ...), custom_call_target="tpu_custom_call" | custom-call | flops 603979776 | bytes 4718592 | tf_op jit(solution)/shard_map/base_values/pallas_call | solution.py:87
  51.5 2.5 %stage.9.refs_7_ = bf16[1024,128]{1,0:T(8,128)(2,1)S(1)} custom-call(s32[96]{0:T(128)S(1)} %copy-done.3, s32[96]{0:T(128)S(1)} %copy-done.4, s32[1]{0:T(128)S(6)} %copy.13.refs_2_, bf16[96,128,128]{2,1,0:T(8,128)(2,1)S(1)} %copy-done.1, bf16[1024,128]{1,0:T(8,128)(2,1)S(1)} %collective-permute-done.8.refs_4_, ...), custom_call_target="tpu_custom_call" | custom-call | flops 1610612736 | bytes 3145728 | tf_op jit(solution)/shard_map/stage/pallas_call | solution.py:186
  54.1 0.3 collective-permute-done.6.refs_4_
  54.3 2.8 %stage.10 = (bf16[1024,128]{1,0:T(8,128)(2,1)S(1)}, f32[1024,128]{1,0:T(8,128)S(1)}, f32[1024,128]{1,0:T(8,128)S(1)}, f32[1,128]{1,0:T(1,128)S(1)}) custom-call(s32[96]{0:T(128)S(1)} %copy-done.3, s32[96]{0:T(128)S(1)} %copy-done.4, s32[1]{0:T(128)S(6)} %copy.13.refs_2_, bf16[96,128,128]{2,1,0:T(8,128)(2,1)S(1)} %copy-done.1, ...), custom_call_target="tpu_custom_call" | custom-call | flops 1610612736 | bytes 3145728 | tf_op jit(solution)/shard_map/stage/pallas_call | solution.py:186
  57.2 2.9 %collective-permute-done.10.refs_4_ = bf16[1024,128]{1,0:T(8,128)(2,1)S(1)} collective-permute-done((bf16[1024,128]{1,0:T(8,128)(2,1)S(1)}, bf16[1024,128]{1,0:T(8,128)(2,1)S(1)}, u32[]{:S(2)}, u32[]{:S(2)}) %collective-permute-start.10) | collective-permute-done | bytes 262176 | tf_op jit(solution)/shard_map/ppermute | solution.py:217
  60.0 3.7 %stage.11 = (bf16[1024,128]{1,0:T(8,128)(2,1)}, f32[1024,128]{1,0:T(8,128)S(1)}, f32[1024,128]{1,0:T(8,128)S(1)}, f32[1,128]{1,0:T(1,128)S(1)}, f32[1024,128]{1,...) custom-call(s32[96]{0:T(128)S(1)} %copy-done.3, s32[96]{0:T(128)S(1)} %copy-done.4, s32[1]{0:T(128)S(6)} %copy.13.refs_2_, ...), custom_call_target="tpu_custom_call" | custom-call | flops 1610612736 | bytes 3145728 | tf_op jit(solution)/shard_map/stage/pallas_call | solution.py:186
  63.9 0.1 reduce_sum.9
  64.1 1.9 %pad_maximum_fusion = (f32[1024,384]{1,0:T(8,128)}, f32[1024,384]{1,0:T(8,128)}) fusion(f32[1024,128]{1,0:T(8,128)S(1)} %get-tuple-element.48, f32[1024,128]{1,0:T(8,128)S(1)} %get-tuple-element.47, f32[1024,128]{1,0:T(8,128)S(1)} %get-tuple-element.42, f32[1024,128]{1,0:T(8,128)S(1)} %get-tuple-element.51, f32[1024,128]{1,0:T(8,128)S(1)} %get-tuple-element.50, ...), kind=kLoop, calls=%fused_computation | loop fusion | flops 1572864 | bytes 6291456 | tf_op jit(solution)/shard_map/concatenate | solution.py:264
  65.9 3.5 %collective-permute-done.13 = f32[8]{0:T(128)S(1)} collective-permute-done((f32[8]{0:T(128)S(1)}, f32[8]{0:T(128)S(1)}, u32[]{:S(2)}, u32[]{:S(2)}) %collective-permute-start.13) | collective-permute-done | bytes 64 | tf_op jit(solution)/shard_map/ppermute | solution.py:259
  69.5 3.5 %collective-permute-done.14 = f32[8]{0:T(128)S(1)} collective-permute-done((f32[8]{0:T(128)S(1)}, f32[8]{0:T(128)S(1)}, u32[]{:S(2)}, u32[]{:S(2)}) %collective-permute-start.14) | collective-permute-done | bytes 64 | tf_op jit(solution)/shard_map/ppermute | solution.py:259
  73.0 4.4 %collective-permute-done.15 = f32[8]{0:T(128)S(1)} collective-permute-done((f32[8]{0:T(128)S(1)}, f32[8]{0:T(128)S(1)}, u32[]{:S(2)}, u32[]{:S(2)}) %collective-permute-start.15) | collective-permute-done | bytes 64 | tf_op jit(solution)/shard_map/ppermute | solution.py:259
  77.5 0.5 add_multiply_fusion
  (43 shorter events, 0.8 us)
Async XLA Ops:
  0.6 1.4 %copy-start = (f32[1024,384]{1,0:T(8,128)S(1)}, f32[1024,384]{1,0:T(8,128)}, u32[]{:S(2)}) copy-start(f32[1024,384]{1,0:T(8,128)} %x_ref.5) | copy-start | bytes 4718596
  2.8 27.5 %collective-permute-start.5 = (bf16[1024,128]{1,0:T(8,128)(2,1)}, bf16[1024,128]{1,0:T(8,128)(2,1)}, u32[]{:S(2)}, u32[]{:S(2)}) collective-permute-start(bf16[1024,128]{1,0:T(8,128)(2,1)} %round_group.5.refs_5_.refs_12_), channel_id=1, source_target_pairs={{1,0},{2,1},{3,2},{4,3},{5,4},{6,5},{7,6},{8,7},{9,8},{10,9},{11,1... | collective-permute-start | bytes 786440 | tf_op jit(solution)/shard_map/ppermute | solution.py:219
  8.2 22.1 %collective-permute-start.4 = (bf16[1024,128]{1,0:T(8,128)(2,1)}, bf16[1024,128]{1,0:T(8,128)(2,1)}, u32[]{:S(2)}, u32[]{:S(2)}) collective-permute-start(bf16[1024,128]{1,0:T(8,128)(2,1)} %round_group.5.refs_5_.refs_12_), channel_id=1, source_target_pairs={{0,1},{1,2},{2,3},{3,4},{4,5},{5,6},{6,7},{7,8},{8,9},{9,10},{10,1... | collective-permute-start | bytes 786440 | tf_op jit(solution)/shard_map/ppermute | solution.py:217
  8.9 17.5 %collective-permute-start.3 = (bf16[1024,128]{1,0:T(8,128)(2,1)}, bf16[1024,128]{1,0:T(8,128)(2,1)}, u32[]{:S(2)}, u32[]{:S(2)}) collective-permute-start(bf16[1024,128]{1,0:T(8,128)(2,1)} %round_group.4.refs_5_.refs_11_), channel_id=1, source_target_pairs={{1,0},{2,1},{3,2},{4,3},{5,4},{6,5},{7,6},{8,7},{9,8},{10,9},{11,1... | collective-permute-start | bytes 786440 | tf_op jit(solution)/shard_map/ppermute | solution.py:219
  13.4 13.1 %collective-permute-start.2 = (bf16[1024,128]{1,0:T(8,128)(2,1)}, bf16[1024,128]{1,0:T(8,128)(2,1)}, u32[]{:S(2)}, u32[]{:S(2)}) collective-permute-start(bf16[1024,128]{1,0:T(8,128)(2,1)} %round_group.4.refs_5_.refs_11_), channel_id=1, source_target_pairs={{0,1},{1,2},{2,3},{3,4},{4,5},{5,6},{6,7},{7,8},{8,9},{9,10},{10,1... | collective-permute-start | bytes 786440 | tf_op jit(solution)/shard_map/ppermute | solution.py:217
  13.4 24.1 %collective-permute-start.1 = (bf16[1024,128]{1,0:T(8,128)(2,1)S(1)}, bf16[1024,128]{1,0:T(8,128)(2,1)}, u32[]{:S(2)}, u32[]{:S(2)}) collective-permute-start(bf16[1024,128]{1,0:T(8,128)(2,1)S(1)} %round_group.3.refs_5_.refs_15_), channel_id=1, source_target_pairs={{1,0},{2,1},{3,2},{4,3},{5,4},{6,5},{7,6},{8,7},{9,8},{10,9},{11,1... | collective-permute-start | bytes 786440 | tf_op jit(solution)/shard_map/ppermute | solution.py:219
  17.9 1.4 %copy-start.5 = (f32[1024,384]{1,0:T(8,128)S(1)}, f32[1024,384]{1,0:T(8,128)}, u32[]{:S(2)}) copy-start(f32[1024,384]{1,0:T(8,128)} %param.8) | copy-start | bytes 4718596
  19.3 0.9 %copy-start.6 = (bf16[48,48]{1,0:T(8,128)(2,1)S(1)}, bf16[48,48]{1,0:T(8,128)(2,1)}, u32[]{:S(2)}) copy-start(bf16[48,48]{1,0:T(8,128)(2,1)} %param.13) | copy-start | bytes 13828
  24.2 1.0 %copy-start.2 = (f32[1024,128]{1,0:T(8,128)S(1)}, f32[1024,128]{1,0:T(8,128)}, u32[]{:S(2)}) copy-start(f32[1024,128]{1,0:T(8,128)} %get-tuple-element.57.refs_4_) | copy-start | bytes 1572868
  25.3 1.9 %copy-start.1 = (bf16[96,128,128]{2,1,0:T(8,128)(2,1)S(1)}, bf16[96,128,128]{2,1,0:T(8,128)(2,1)}, u32[]{:S(2)}) copy-start(bf16[96,128,128]{2,1,0:T(8,128)(2,1)} %refs_3_.11) | copy-start | bytes 9437188
  25.3 1.9 %copy-start.3 = (s32[96]{0:T(128)S(1)}, s32[96]{0:T(128)}, u32[]{:S(2)}) copy-start(s32[96]{0:T(128)} %refs_0_.11) | copy-start | bytes 1156
  25.3 1.9 %copy-start.4 = (s32[96]{0:T(128)S(1)}, s32[96]{0:T(128)}, u32[]{:S(2)}) copy-start(s32[96]{0:T(128)} %refs_1_.11) | copy-start | bytes 1156
  26.4 11.1 %collective-permute-start = (bf16[1024,128]{1,0:T(8,128)(2,1)S(1)}, bf16[1024,128]{1,0:T(8,128)(2,1)S(1)}, u32[]{:S(2)}, u32[]{:S(2)}) collective-permute-start(bf16[1024,128]{1,0:T(8,128)(2,1)S(1)} %round_group.3.refs_5_.refs_15_), channel_id=1, source_target_pairs={{0,1},{1,2},{2,3},{3,4},{4,5},{5,6},{6,7},{7,8},{8,9},{9,10},{10,1... | collective-permute-start | bytes 786440 | tf_op jit(solution)/shard_map/ppermute | solution.py:217
  33.7 17.8 %collective-permute-start.9 = (bf16[1024,128]{1,0:T(8,128)(2,1)S(1)}, bf16[1024,128]{1,0:T(8,128)(2,1)S(1)}, u32[]{:S(2)}, u32[]{:S(2)}) collective-permute-start(bf16[1024,128]{1,0:T(8,128)(2,1)S(1)} %get-tuple-element.34.refs_5_.refs_11_), channel_id=1, source_target_pairs={{1,0},{2,1},{3,2},{4,3},{5,4},{6,5},{7,6},{8,7},{9,8},{10,9},{11,1... | collective-permute-start | bytes 786440 | tf_op jit(solution)/shard_map/ppermute | solution.py:219
  37.5 14.0 %collective-permute-start.8 = (bf16[1024,128]{1,0:T(8,128)(2,1)S(1)}, bf16[1024,128]{1,0:T(8,128)(2,1)S(1)}, u32[]{:S(2)}, u32[]{:S(2)}) collective-permute-start(bf16[1024,128]{1,0:T(8,128)(2,1)S(1)} %get-tuple-element.34.refs_5_.refs_11_), channel_id=1, source_target_pairs={{0,1},{1,2},{2,3},{3,4},{4,5},{5,6},{6,7},{7,8},{8,9},{9,10},{10,1... | collective-permute-start | bytes 786440 | tf_op jit(solution)/shard_map/ppermute | solution.py:217
  41.4 12.7 %collective-permute-start.7 = (bf16[1024,128]{1,0:T(8,128)(2,1)S(1)}, bf16[1024,128]{1,0:T(8,128)(2,1)S(1)}, u32[]{:S(2)}, u32[]{:S(2)}) collective-permute-start(bf16[1024,128]{1,0:T(8,128)(2,1)S(1)} %get-tuple-element.33.refs_5_.refs_12_), channel_id=1, source_target_pairs={{1,0},{2,1},{3,2},{4,3},{5,4},{6,5},{7,6},{8,7},{9,8},{10,9},{11,1... | collective-permute-start | bytes 786440 | tf_op jit(solution)/shard_map/ppermute | solution.py:219
  45.8 8.5 %collective-permute-start.6 = (bf16[1024,128]{1,0:T(8,128)(2,1)S(1)}, bf16[1024,128]{1,0:T(8,128)(2,1)S(1)}, u32[]{:S(2)}, u32[]{:S(2)}) collective-permute-start(bf16[1024,128]{1,0:T(8,128)(2,1)S(1)} %get-tuple-element.33.refs_5_.refs_12_), channel_id=1, source_target_pairs={{0,1},{1,2},{2,3},{3,4},{4,5},{5,6},{6,7},{7,8},{8,9},{9,10},{10,1... | collective-permute-start | bytes 786440 | tf_op jit(solution)/shard_map/ppermute | solution.py:217
  45.8 11.3 %collective-permute-start.11 = (bf16[1024,128]{1,0:T(8,128)(2,1)S(1)}, bf16[1024,128]{1,0:T(8,128)(2,1)S(1)}, u32[]{:S(2)}, u32[]{:S(2)}) collective-permute-start(bf16[1024,128]{1,0:T(8,128)(2,1)S(1)} %get-tuple-element.43.refs_5_.refs_15_), channel_id=1, source_target_pairs={{1,0},{2,1},{3,2},{4,3},{5,4},{6,5},{7,6},{8,7},{9,8},{10,9},{11,1... | collective-permute-start | bytes 786440 | tf_op jit(solution)/shard_map/ppermute | solution.py:219
  51.5 8.5 %collective-permute-start.10 = (bf16[1024,128]{1,0:T(8,128)(2,1)S(1)}, bf16[1024,128]{1,0:T(8,128)(2,1)S(1)}, u32[]{:S(2)}, u32[]{:S(2)}) collective-permute-start(bf16[1024,128]{1,0:T(8,128)(2,1)S(1)} %get-tuple-element.43.refs_5_.refs_15_), channel_id=1, source_target_pairs={{0,1},{1,2},{2,3},{3,4},{4,5},{5,6},{6,7},{7,8},{8,9},{9,10},{10,1... | collective-permute-start | bytes 786440 | tf_op jit(solution)/shard_map/ppermute | solution.py:217
  64.0 1.9 %collective-permute-start.12 = (f32[8]{0:T(128)S(1)}, f32[8]{0:T(128)S(1)}, u32[]{:S(2)}, u32[]{:S(2)}) collective-permute-start(f32[8]{0:T(128)S(1)} %reduce_sum.9), channel_id=1, source_target_pairs={{0,1},{1,0},{2,3},{3,2},{4,5},{5,4},{6,7},{7,6},{8,9},{9,8},{10,11... | collective-permute-start | bytes 104 | tf_op jit(solution)/shard_map/ppermute | solution.py:259
  65.9 3.5 %collective-permute-start.13 = (f32[8]{0:T(128)S(1)}, f32[8]{0:T(128)S(1)}, u32[]{:S(2)}, u32[]{:S(2)}) collective-permute-start(f32[8]{0:T(128)S(1)} %add.12), channel_id=1, source_target_pairs={{0,2},{1,3},{2,0},{3,1},{4,6},{5,7},{6,4},{7,5},{8,10},{9,11},{10,... | collective-permute-start | bytes 104 | tf_op jit(solution)/shard_map/ppermute | solution.py:259
  69.5 3.5 %collective-permute-start.14 = (f32[8]{0:T(128)S(1)}, f32[8]{0:T(128)S(1)}, u32[]{:S(2)}, u32[]{:S(2)}) collective-permute-start(f32[8]{0:T(128)S(1)} %add.13), channel_id=1, source_target_pairs={{0,4},{1,5},{2,6},{3,7},{4,0},{5,1},{6,2},{7,3},{8,12},{9,13},{10,... | collective-permute-start | bytes 104 | tf_op jit(solution)/shard_map/ppermute | solution.py:259
  73.0 4.4 %collective-permute-start.15 = (f32[8]{0:T(128)S(1)}, f32[8]{0:T(128)S(1)}, u32[]{:S(2)}, u32[]{:S(2)}) collective-permute-start(f32[8]{0:T(128)S(1)} %add.14), channel_id=1, source_target_pairs={{0,8},{1,9},{2,10},{3,11},{4,12},{5,13},{6,14},{7,15},{8,0},{9,1},... | collective-permute-start | bytes 104 | tf_op jit(solution)/shard_map/ppermute | solution.py:259
where the time goes:
time: 78.3 us; the launch traced here: 78 us
  starting transfers between devices  27.3 us (35%)
  Pallas kernels  23.3 us (30%)
  waiting for transfers between devices  14.7 us (19%)
  local copies, waits for them, and re-layouts  7.79 us (10%)
  other arithmetic  3.54 us (5%)
  between operations  1.46 us (2%)
    ppermute x6, starting transfers between devices, exchange(): lax.ppermute(mine, ('row', 'col'), back)  27.1 us
    pallas_call x6, Pallas kernels, stage(): pl.pallas_call(body, in_specs=[SMEM_SPEC] * 3 + [VMEM_SPEC] * (5 + len(ke...  19.4 us
    ppermute x4, waiting for transfers between devices, local(): lax.ppermute(partial, ('row', 'col'), [(i, i ^ size) for i in range(ring)])  11.5 us
    unnamed x14, local copies, waits for them, and re-layouts  4.38 us
    ppermute x6, waiting for transfers between devices, exchange(): lax.ppermute(mine, ('row', 'col'), ahead)  3.14 us
    pallas_call x2, Pallas kernels, base_values(): pl.pallas_call(body, in_specs=[VMEM_SPEC] * (2 * groups + 1), out_specs=[...  2.36 us
    concatenate x1, other arithmetic, local(): return (jnp.concatenate(xs, axis=1), jnp.concatenate(ys, axis=1), energy)  1.87 us
    mul x1, local copies, waits for them, and re-layouts, local(): eye[:, None, :, None] * channel_coupling[None, :, None, :]  1.83 us
  transfers between devices with their start and end apart: 16, of which 5 were waited for; matrix products, arithmetic and copies ran while one was open for 8% of the time, Pallas kernels for 24%

commit v1 on v0

v1 whole, which is shorter than its diff:
```python
import jax
import jax.numpy as jnp
import ml_dtypes
import numpy as np
from jax import lax
from jax.experimental import pallas as pl
from jax.experimental.pallas import tpu as pltpu
from jax.sharding import PartitionSpec as P

STEPS = 2
LANES = 128
UNROLL = 16
VMEM_LIMIT = 40 * 1024 * 1024
F32 = jnp.float32
BF16 = jnp.bfloat16

SMEM = pl.BlockSpec(memory_space=pltpu.SMEM)
VMEM = pl.BlockSpec(memory_space=pltpu.VMEM)
HBM = pl.BlockSpec(memory_space=pltpu.HBM)


def params():
    return pltpu.CompilerParams(vmem_limit_bytes=VMEM_LIMIT)


def cost(flops, moved):
    return pl.CostEstimate(flops=int(flops), bytes_accessed=int(moved), transcendentals=0)


def shape(rows, columns, dtype):
    return jax.ShapeDtypeStruct((rows, columns), dtype)


def lanes(group):
    return slice(group * LANES, (group + 1) * LANES)


def spanned(group, channels, width):
    first = group * LANES // channels * channels
    last = -(-(group + 1) * LANES // channels) * channels
    return list(range(first // LANES, -(-min(last, width) // LANES)))


def span_lanes(near):
    return slice(near[0] * LANES, (near[-1] + 1) * LANES)


def detune(step):
    return 1.0 - (step + 1.0) / (STEPS + 1.0)


def round_first(positions):
    cells = positions.shape[0]

    def body(x_ref, out_ref, buf, sem):
        copy = pltpu.make_async_copy(x_ref.at[:, lanes(0)], buf, sem)
        copy.start()
        copy.wait()
        out_ref[...] = buf[...].astype(BF16)

    return pl.pallas_call(
        body,
        in_specs=[HBM],
        out_specs=VMEM,
        out_shape=shape(cells, LANES, BF16),
        scratch_shapes=[pltpu.VMEM((cells, LANES), F32), pltpu.SemaphoreType.DMA],
        compiler_params=params(),
        cost_estimate=cost(0, cells * LANES * 6),
        name="round_first",
    )(positions)


def totals_of(high, low, same, near, group):
    ones = same[span_lanes(near), lanes(group)]
    return jnp.dot(
        jnp.concatenate([high[n] for n in near], axis=1), ones, preferred_element_type=F32
    ) + jnp.dot(jnp.concatenate([low[n] for n in near], axis=1), ones, preferred_element_type=F32)


def base_of(x, y, totals, step, channels):
    penalty = 0.02 * (totals - (2.0 - channels))
    return y + 0.5 * (-detune(step) * x - 0.4 * penalty)


def split(x):
    high = x.astype(BF16)
    return high, (x - high.astype(F32)).astype(BF16)


def prepare(positions, momenta, same, spread, coupling, emit):
    cells, width = positions.shape
    channels = coupling.shape[0]
    groups = width // LANES

    def body(x_ref, y_ref, same_ref, spread_ref, coupling_ref, *outs):
        mixing_out, base_outs, round_outs = outs[0], outs[1 : 1 + groups], outs[1 + groups :]
        x = [x_ref[:, lanes(g)] for g in range(groups)]
        parts = [split(v) for v in x]
        for out, g in zip(round_outs, emit):
            out[...] = parts[g][0]
        tall = jnp.dot(
            spread_ref[...], coupling_ref[...], preferred_element_type=F32
        ).astype(BF16)
        wide = lax.dot_general(
            tall, spread_ref[...], (((1,), (1,)), ((), ())), preferred_element_type=F32
        )
        mixing_out[...] = (wide * same_ref[...].astype(F32)).astype(BF16)
        for g in range(groups):
            near = spanned(g, channels, width)
            totals = totals_of([p[0] for p in parts], [p[1] for p in parts], same_ref, near, g)
            base_outs[g][...] = base_of(x[g], y_ref[:, lanes(g)], totals, 0, channels)

    outs = pl.pallas_call(
        body,
        in_specs=[VMEM] * 5,
        out_specs=[VMEM] * (1 + groups + len(emit)),
        out_shape=[shape(width, width, BF16)]
        + [shape(cells, LANES, F32)] * groups
        + [shape(cells, LANES, BF16)] * len(emit),
        compiler_params=params(),
        cost_estimate=cost(4 * cells * width * width, cells * width * 12),
        name="prepare",
    )(positions, momenta, same, spread, coupling)
    return outs[0], outs[1 : 1 + groups], outs[1 + groups :]


def field_into(rows, cols, count, tiles, parts, field, window):
    slots, tile, _ = tiles.shape
    spare = field.shape[0] - 1
    per = window.shape[0] // len(parts)
    for k, part in enumerate(parts):
        window[k * per : (k + 1) * per] = part[...].reshape(per, tile, LANES)
    field[...] = jnp.zeros_like(field)
    live = count[0]

    def some(start, unroll):
        for u in range(unroll):
            slot = start + u
            row = jnp.where(slot < live, rows[slot], spare)
            field[row] += jnp.dot(tiles[slot], window[cols[slot]], preferred_element_type=F32)

    whole = slots // UNROLL

    def body(i, carry):
        some(i * UNROLL, UNROLL)
        return carry

    lax.fori_loop(0, whole, body, 0)
    some(whole * UNROLL, slots - whole * UNROLL)


def stage(
    slot_args, channels, mixing, group, parts, before=(), after=(), mix=(), rounds=(), name="stage"
):
    rows, cols, count, tiles = slot_args
    slots, tile, _ = tiles.shape
    cells = parts[0].shape[0]
    width = mixing.shape[0]
    per = cells // tile
    arrays, shapes = [], []

    def take(array):
        for i, held in enumerate(arrays):
            if held is array:
                return i
        arrays.append(array)
        return len(arrays) - 1

    def give(*kinds):
        shapes.extend(shape(n, LANES, kind) for n, kind in kinds)
        return list(range(len(shapes) - len(kinds), len(shapes)))

    def near_fields(t, fields):
        near = spanned(t, channels, width)
        return [None if fields[n] is None else take(fields[n]) for n in near]

    part_ids = [take(p) for p in parts]
    mixing_id = take(mixing)
    (own_out,) = give((cells, BF16))
    jobs = [
        [
            (t, near_fields(t, fields), take(base), take(x), where, give(*[(cells, k) for k in (F32, F32, BF16)]))
            for t, fields, base, x, where in todo
        ]
        for todo in (before, after)
    ]
    mix_jobs = [
        (t, near_fields(t, fields), take(rounded), give((cells, F32), (1, F32)))
        for t, fields, rounded in mix
    ]
    round_jobs = [(take(x), where, give((cells, BF16))) for x, where in rounds]
    n_in, n_out = len(arrays), len(shapes)

    def body(rows_ref, cols_ref, count_ref, tiles_ref, *refs):
        ins, outs, (field, window) = refs[:n_in], refs[n_in : n_in + n_out], refs[n_in + n_out :]

        def mixed_of(t, ids, own):
            near = spanned(t, channels, width)
            return jnp.dot(
                jnp.concatenate([own if i is None else ins[i][...] for i in ids], axis=1),
                ins[mixing_id][span_lanes(near), lanes(t)],
                preferred_element_type=F32,
            )

        def update(job, own):
            t, ids, base, x, where, (x_out, y_out, r_out) = job
            y_new = ins[base][...] - 0.2 * mixed_of(t, ids, own)
            x_new = jnp.clip(ins[x][:, where] + 0.5 * y_new, -1.0, 1.0)
            outs[x_out][...] = x_new
            outs[y_out][...] = y_new
            outs[r_out][...] = x_new.astype(BF16)

        for job in jobs[0]:
            update(job, None)
        for x, where, (out,) in round_jobs:
            outs[out][...] = ins[x][:, where].astype(BF16)
        field_into(
            rows_ref, cols_ref, count_ref, tiles_ref, [ins[i] for i in part_ids], field, window
        )
        own = field[:per].reshape(cells, LANES).astype(BF16)
        outs[own_out][...] = own
        for job in jobs[1]:
            update(job, own)
        for t, ids, rounded, (mixed_out, energy_out) in mix_jobs:
            mixed = mixed_of(t, ids, own)
            outs[mixed_out][...] = mixed
            outs[energy_out][...] = jnp.sum(
                ins[rounded][...].astype(F32) * mixed, axis=0, keepdims=True
            )

    outs = pl.pallas_call(
        body,
        in_specs=[SMEM] * 3 + [VMEM] * (1 + n_in),
        out_specs=[VMEM] * n_out,
        out_shape=shapes,
        scratch_shapes=[
            pltpu.VMEM((per + 1, tile, LANES), F32),
            pltpu.VMEM((3 * per, tile, LANES), BF16),
        ],
        compiler_params=params(),
        cost_estimate=cost(8 * slots * tile * tile * LANES, slots * tile * tile * 2),
        name=name,
    )(rows, cols, count, tiles, *arrays)
    return (
        outs[own_out],
        [[outs[i] for i in job[-1]] for job in jobs[0] + jobs[1]],
        [[outs[i] for i in job[-1]] for job in mix_jobs],
        [outs[job[-1][0]] for job in round_jobs],
    )


def finish(xs, ys, mixed, same, channels):
    groups = len(xs)
    cells = xs[0].shape[0]
    width = groups * LANES
    block = cells // 4 if cells % 64 == 0 else cells

    def body(*refs):
        x_refs, y_refs, mixed_refs = [refs[i * groups : (i + 1) * groups] for i in range(3)]
        same_ref, x_out, y_out = refs[3 * groups :]
        x = [r[...] for r in x_refs]
        parts = [split(v) for v in x]
        for g in range(groups):
            near = spanned(g, channels, width)
            totals = totals_of([p[0] for p in parts], [p[1] for p in parts], same_ref, near, g)
            base = base_of(x[g], y_refs[g][...], totals, STEPS - 1, channels)
            y_new = base - 0.2 * mixed_refs[g][...]
            y_out[:, lanes(g)] = y_new
            x_out[:, lanes(g)] = jnp.clip(x[g] + 0.5 * y_new, -1.0, 1.0)

    part = pl.BlockSpec((block, LANES), lambda i: (i, 0))
    full = pl.BlockSpec((block, width), lambda i: (i, 0))
    return pl.pallas_call(
        body,
        grid=(cells // block,),
        in_specs=[part] * (3 * groups) + [pl.BlockSpec((width, width), lambda i: (0, 0))],
        out_specs=[full, full],
        out_shape=[shape(cells, width, F32)] * 2,
        compiler_params=params(),
        cost_estimate=cost(4 * cells * width * width, cells * width * 12),
        name="finish",
    )(*xs, *ys, *mixed, same)


def sum_over_ring(value, ring):
    if ring & (ring - 1):
        return lax.psum(value, ("row", "col"))
    size = 1
    while size < ring:
        digits = (1, 2, 3) if 4 * size <= ring else (1,)
        value = value + sum(
            lax.ppermute(value, ("row", "col"), [(i, i ^ (size * d)) for i in range(ring)])
            for d in digits
        )
        size *= len(digits) + 1
    return value


def local(positions, momenta, tile_values, tile_rows, tile_cols, tile_count, channel_coupling):
    cells, width = positions.shape
    channels = channel_coupling.shape[0]
    replicas = width // channels
    groups = width // LANES
    ring = lax.axis_size("row") * lax.axis_size("col")
    where = np.arange(width)
    same = (where[:, None] // channels == where[None] // channels).astype(ml_dtypes.bfloat16)
    spread = (where[:, None] % channels == np.arange(channels)[None]).astype(ml_dtypes.bfloat16)
    slot_args = (tile_rows, tile_cols, tile_count, tile_values)
    ahead = [(i, (i + 1) % ring) for i in range(ring)]
    back = [((i + 1) % ring, i) for i in range(ring)]

    def exchange(mine):
        return [
            lax.ppermute(mine, ("row", "col"), ahead),
            mine,
            lax.ppermute(mine, ("row", "col"), back),
        ]

    ready = {g: [] for g in range(groups)}
    for g in range(groups):
        ready[max(spanned(g, channels, width))].append(g)

    def fields_for(t, known, own):
        return {n: None if n == own else known[n] for n in spanned(t, channels, width)}

    first = round_first(positions)
    windows = [exchange(first)]
    emit = [1] if groups > 1 else []
    mixing, bases, early = prepare(positions, momenta, same, spread, channel_coupling, emit)
    windows += [exchange(r) for r in early]
    known, state, waiting = {}, {}, []
    for g in range(groups):
        waiting += ready[g]
        now, waiting = waiting[:1], waiting[1:]
        coming = [len(windows)] if len(windows) < groups else []
        known[g], updated, _, rounded = stage(
            slot_args,
            channels,
            mixing,
            g,
            windows[g],
            after=[(t, fields_for(t, known, g), bases[t], positions, lanes(t)) for t in now],
            rounds=[(positions, lanes(c)) for c in coming],
            name=f"first_{g}",
        )
        state.update(zip(now, updated))
        windows += [exchange(r) for r in rounded]
    new_windows = {t: exchange(state[t][2]) for t in state}
    last_known, mixed, energies = {}, {}, {}
    for g in range(groups):
        now, waiting = waiting[:1], waiting[1:]
        last_known[g], updated, mixes, _ = stage(
            slot_args,
            channels,
            mixing,
            g,
            new_windows[g],
            before=[(t, fields_for(t, known, None), bases[t], positions, lanes(t)) for t in now],
            mix=[(t, fields_for(t, last_known, g), state[t][2]) for t in ready[g]],
            name=f"second_{g}",
        )
        for t, new in zip(now, updated):
            state[t] = new
            new_windows[t] = exchange(new[2])
        for t, (field, energy) in zip(ready[g], mixes):
            mixed[t], energies[t] = field, energy
    partial = jnp.concatenate([energies[g] for g in range(groups)], axis=1)
    partial = partial.reshape(replicas, channels).sum(axis=1)
    energy = sum_over_ring(partial, ring) / jnp.sqrt(jnp.float32(cells * ring * channels))
    x_new, y_new = finish(
        [state[g][0] for g in range(groups)],
        [state[g][1] for g in range(groups)],
        [mixed[g] for g in range(groups)],
        same,
        channels,
    )
    return (x_new, y_new, energy)


def solution(mesh):
    cells = P(("groups", "row", "col"), None)
    slots = P(("groups", "row", "col"))
    return jax.shard_map(
        local,
        mesh=mesh,
        in_specs=(cells, cells, P(("groups", "row", "col"), None, None), slots, slots, slots, P()),
        out_specs=(cells, cells, P("groups")),
        check_vma=False,
    )
```

time: 78.3 us -> 72.4 us (0.925)
  waiting for transfers between devices: 14.7 us -> 5.41 us
  starting transfers between devices: 27.3 us -> 34.4 us
  other arithmetic: 3.54 us -> 0.66 us
  Pallas kernels: 23.3 us -> 22.2 us
    ppermute x4 -> x6, waiting for transfers between devices: 11.5 us -> 5.06 us  [sum_over_ring(): lax.ppermute(value, ('row', 'col'), [(i, i ^ size * d) for i in range(rin...]
    ppermute x4 -> x6, starting transfers between devices: 0.07 us -> 6.36 us  [sum_over_ring(): lax.ppermute(value, ('row', 'col'), [(i, i ^ size * d) for i in range(rin...]
    unnamed x14 -> x30, local copies, waits for them, and re-layouts: 4.38 us -> 7.88 us
    ppermute x6, waiting for transfers between devices: 3.14 us -> 0.33 us  [exchange(): lax.ppermute(mine, ('row', 'col'), ahead)]
    concatenate x2 -> x1, other arithmetic: 1.89 us -> 0.02 us  [local(): partial = jnp.concatenate([energies[g] for g in range(groups)], axis=1)]
    mul x1 -> x0, local copies, waits for them, and re-layouts: 1.83 us -> none  [local(): eye[:, None, :, None] * channel_coupling[None, :, None, :]]
    pallas_call x11 -> x9, Pallas kernels: 23.3 us -> 22.2 us  [the longest x6 17.6 us: stage(): pl.pallas_call(body, in_specs=[SMEM] * 3 + [VMEM] * (1 + n_in), out_specs...]
    mul x1 -> x0, other arithmetic: 1 us -> none  [local(): eye[:, None, :, None] * channel_coupling[None, :, None, :]]
  transfers between devices with their start and end apart: 16 -> 18, of which waited for: 5 -> 3; matrix products, arithmetic and copies ran while one was open for 8% -> 0% of each run, Pallas kernels for 24% -> 26%
where the time goes in v1:
time: 72.4 us; the launch traced here: 72.1 us
  starting transfers between devices  34.4 us (48%)
  Pallas kernels  22.2 us (31%)
  local copies, waits for them, and re-layouts  7.96 us (11%)
  waiting for transfers between devices  5.41 us (7%)
  between operations  1.51 us (2%)
    ppermute x6, starting transfers between devices, exchange(): lax.ppermute(mine, ('row', 'col'), back)  27.2 us
    pallas_call x6, Pallas kernels, stage(): pl.pallas_call(body, in_specs=[SMEM] * 3 + [VMEM] * (1 + n_in), out_specs...  17.6 us
    unnamed x30, local copies, waits for them, and re-layouts  7.88 us
    ppermute x6, starting transfers between devices, sum_over_ring(): lax.ppermute(value, ('row', 'col'), [(i, i ^ size * d) for i in range(rin...  6.36 us
    ppermute x6, waiting for transfers between devices, sum_over_ring(): lax.ppermute(value, ('row', 'col'), [(i, i ^ size * d) for i in range(rin...  5.06 us
    pallas_call x1, Pallas kernels, finish(): pl.pallas_call(body, grid=(cells // block,), in_specs=[part] * (3 * group...  3.13 us
  transfers between devices with their start and end apart: 18, of which 3 were waited for; matrix products, arithmetic and copies ran while one was open for 0% of the time, Pallas kernels for 26%

profile of v1, /device:TPU:0, one launch (start us, length us, event | category | flops | bytes accessed | tf_op | source)
XLA Modules:
  0.0 72.1 jit_solution(13389211005223190557)
XLA Ops:
  0.6 1.4 %copy-done = f32[1024,384]{1,0:T(8,128)S(1)} copy-done((f32[1024,384]{1,0:T(8,128)S(1)}, f32[1024,384]{1,0:T(8,128)}, u32[]{:S(2)}) %copy-start) | copy-done | bytes 1572888
  2.2 0.5 collective-permute-start.2
  2.7 5.1 %collective-permute-start.3 = (bf16[1024,128]{1,0:T(8,128)(2,1)S(1)}, bf16[1024,128]{1,0:T(8,128)(2,1)S(1)}, u32[]{:S(2)}, u32[]{:S(2)}) collective-permute-start(bf16[1024,128]{1,0:T(8,128)(2,1)S(1)} %round_first.1.refs_1_), channel_id=1, source_target_pairs={{1,0},{2,1},{3,2},{4,3},{5,4},{6,5},{7,6},{8,7},{9,8},{10,9},{11,1... | collective-permute-start | bytes 786440 | tf_op jit(solution)/shard_map/ppermute | solution.py:316
  7.7 1.0 %copy-done.3 = bf16[384,384]{1,0:T(8,128)(2,1)S(1)} copy-done((bf16[384,384]{1,0:T(8,128)(2,1)S(1)}, bf16[384,384]{1,0:T(8,128)(2,1)}, u32[]{:S(2)}) %copy-start.3) | copy-done | bytes 294936
  8.7 1.4 %prepare.1 = (bf16[384,384]{1,0:T(8,128)(2,1)S(1)}, f32[1024,128]{1,0:T(8,128)S(1)}, f32[1024,128]{1,0:T(8,128)S(1)}, f32[1024,128]{1,0:T(8,128)S(1)}, bf16[1024,128]{1,0:T(8,128)(2,1)S(1)}) custom-call(f32[1024,384]{1,0:T(8,128)S(1)} %copy-done, f32[1024,384]{1,0:T(8,128)S(1)} %copy-done.2, bf16[384,384]{1,0:T(8,128)(2,1)S(1)} %copy-done.3, ...), custom_call_target="tpu_custom_call" | custom-call | flops 603979776 | bytes 4718592 | tf_op jit(solution)/shard_map/prepare/pallas_call | solution.py:113
  10.2 4.4 %collective-permute-start.1 = (bf16[1024,128]{1,0:T(8,128)(2,1)S(1)}, bf16[1024,128]{1,0:T(8,128)(2,1)S(1)}, u32[]{:S(2)}, u32[]{:S(2)}) collective-permute-start(bf16[1024,128]{1,0:T(8,128)(2,1)S(1)} %get-tuple-element.31.refs_1_), channel_id=1, source_target_pairs={{1,0},{2,1},{3,2},{4,3},{5,4},{6,5},{7,6},{8,7},{9,8},{10,9},{11,1... | collective-permute-start | bytes 786440 | tf_op jit(solution)/shard_map/ppermute | solution.py:316
  15.3 2.6 %first_0.1 = (bf16[1024,128]{1,0:T(8,128)(2,1)S(1)}, bf16[1024,128]{1,0:T(8,128)(2,1)S(1)}) custom-call(s32[96]{0:T(128)S(1)} %copy-done.13, s32[96]{0:T(128)S(1)} %copy-done.14, s32[1]{0:T(128)S(6)} %copy.12.count_ref, bf16[96,128,128]{2,1,0:T(8,128)(2,1)S(1)} %copy-done.1, bf16[1024,128]{1,0:T(8,128)(2,1)S(1)} %collective-permute-done.2.refs_0_, ...), custom_call_target="tpu_custom_call" | custom-call | flops 1610612736 | bytes 3145728 | tf_op jit(solution)/shard_map/first_0/pallas_call | solution.py:231
  18.0 4.4 %collective-permute-start.5 = (bf16[1024,128]{1,0:T(8,128)(2,1)S(1)}, bf16[1024,128]{1,0:T(8,128)(2,1)S(1)}, u32[]{:S(2)}, u32[]{:S(2)}) collective-permute-start(bf16[1024,128]{1,0:T(8,128)(2,1)S(1)} %get-tuple-element.36.refs_1_), channel_id=1, source_target_pairs={{1,0},{2,1},{3,2},{4,3},{5,4},{6,5},{7,6},{8,7},{9,8},{10,9},{11,1... | collective-permute-start | bytes 786440 | tf_op jit(solution)/shard_map/ppermute | solution.py:316
  22.4 2.9 %first_1.1 = (bf16[1024,128]{1,0:T(8,128)(2,1)S(1)}, f32[1024,128]{1,0:T(8,128)S(1)}, f32[1024,128]{1,0:T(8,128)S(1)}, bf16[1024,128]{1,0:T(8,128)(2,1)S(1)}) custom-call(s32[96]{0:T(128)S(1)} %copy-done.13, s32[96]{0:T(128)S(1)} %copy-done.14, s32[1]{0:T(128)S(6)} %copy.12.count_ref, bf16[96,128,128]{2,1,0:T(8,128)(2,1)S(1)} %copy-done.1, ...), custom_call_target="tpu_custom_call" | custom-call | flops 1610612736 | bytes 3145728 | tf_op jit(solution)/shard_map/first_1/pallas_call | solution.py:231
  25.4 4.4 %collective-permute-start.7 = (bf16[1024,128]{1,0:T(8,128)(2,1)S(1)}, bf16[1024,128]{1,0:T(8,128)(2,1)S(1)}, u32[]{:S(2)}, u32[]{:S(2)}) collective-permute-start(bf16[1024,128]{1,0:T(8,128)(2,1)S(1)} %get-tuple-element.40.refs_1_.refs_5_), channel_id=1, source_target_pairs={{1,0},{2,1},{3,2},{4,3},{5,4},{6,5},{7,6},{8,7},{9,8},{10,9},{11,1... | collective-permute-start | bytes 786440 | tf_op jit(solution)/shard_map/ppermute | solution.py:316
  29.8 3.0 %first_2.1 = (bf16[1024,128]{1,0:T(8,128)(2,1)S(1)}, f32[1024,128]{1,0:T(8,128)S(1)}, f32[1024,128]{1,0:T(8,128)S(1)}, bf16[1024,128]{1,0:T(8,128)(2,1)S(1)}) custom-call(s32[96]{0:T(128)S(1)} %copy-done.13, s32[96]{0:T(128)S(1)} %copy-done.14, s32[1]{0:T(128)S(6)} %copy.12.count_ref, bf16[96,128,128]{2,1,0:T(8,128)(2,1)S(1)} %copy-done.1, ...), custom_call_target="tpu_custom_call" | custom-call | flops 1610612736 | bytes 3145728 | tf_op jit(solution)/shard_map/first_2/pallas_call | solution.py:231
  32.8 4.4 %collective-permute-start.9 = (bf16[1024,128]{1,0:T(8,128)(2,1)S(1)}, bf16[1024,128]{1,0:T(8,128)(2,1)S(1)}, u32[]{:S(2)}, u32[]{:S(2)}) collective-permute-start(bf16[1024,128]{1,0:T(8,128)(2,1)S(1)} %get-tuple-element.47.refs_1_.refs_6_), channel_id=1, source_target_pairs={{1,0},{2,1},{3,2},{4,3},{5,4},{6,5},{7,6},{8,7},{9,8},{10,9},{11,1... | collective-permute-start | bytes 786440 | tf_op jit(solution)/shard_map/ppermute | solution.py:316
  37.3 2.9 %second_0.1 = (bf16[1024,128]{1,0:T(8,128)(2,1)S(1)}, f32[1024,128]{1,0:T(8,128)S(1)}, f32[1024,128]{1,0:T(8,128)S(1)}, bf16[1024,128]{1,0:T(8,128)(2,1)S(1)}) custom-call(s32[96]{0:T(128)S(1)} %copy-done.13, s32[96]{0:T(128)S(1)} %copy-done.14, s32[1]{0:T(128)S(6)} %copy.12.count_ref, bf16[96,128,128]{2,1,0:T(8,128)(2,1)S(1)} %copy-done.1, ...), custom_call_target="tpu_custom_call" | custom-call | flops 1610612736 | bytes 3145728 | tf_op jit(solution)/shard_map/second_0/pallas_call | solution.py:231
  40.2 4.4 %collective-permute-start.11 = (bf16[1024,128]{1,0:T(8,128)(2,1)S(1)}, bf16[1024,128]{1,0:T(8,128)(2,1)S(1)}, u32[]{:S(2)}, u32[]{:S(2)}) collective-permute-start(bf16[1024,128]{1,0:T(8,128)(2,1)S(1)} %get-tuple-element.50.refs_1_), channel_id=1, source_target_pairs={{1,0},{2,1},{3,2},{4,3},{5,4},{6,5},{7,6},{8,7},{9,8},{10,9},{11,1... | collective-permute-start | bytes 786440 | tf_op jit(solution)/shard_map/ppermute | solution.py:316
  44.6 2.9 %second_1.1 = (bf16[1024,128]{1,0:T(8,128)(2,1)S(1)}, f32[1024,128]{1,0:T(8,128)S(1)}, f32[1,128]{1,0:T(1,128)S(1)}) custom-call(s32[96]{0:T(128)S(1)} %copy-done.13, s32[96]{0:T(128)S(1)} %copy-done.14, s32[1]{0:T(128)S(6)} %copy.12.count_ref, bf16[96,128,128]{2,1,0:T(8,128)(2,1)S(1)} %copy-done.1, bf16[1024,128]{1,0:T(8,128)(2,1)S(1)} %collective-permute-done.8.refs_0_, ...), custom_call_target="tpu_custom_call" | custom-call | flops 1610612736 | bytes 3145728 | tf_op jit(solution)/shard_map/second_1/pallas_call | solution.py:231
  47.6 0.8 %copy-done.5 = f32[1024,128]{1,0:T(8,128)} copy-done((f32[1024,128]{1,0:T(8,128)}, f32[1024,128]{1,0:T(8,128)S(1)}, u32[]{:S(2)}) %copy-start.5) | copy-done | bytes 524312
  48.4 0.3 collective-permute-done.10.refs_0_
  48.7 3.4 %second_2.1 = (bf16[1024,128]{1,0:T(8,128)(2,1)}, f32[1024,128]{1,0:T(8,128)S(1)}, f32[1,128]{1,0:T(1,128)S(1)}, f32[1024,128]{1,0:T(8,128)S(1)}, f32[1,128]{1,0:T(1,128)S(1)}) custom-call(s32[96]{0:T(128)S(1)} %copy-done.13, s32[96]{0:T(128)S(1)} %copy-done.14, s32[1]{0:T(128)S(6)} %copy.12.count_ref, bf16[96,128,128]{2,1,0:T(8,128)(2,1)S(1)} %copy-done.1, ...), custom_call_target="tpu_custom_call" | custom-call | flops 1610612736 | bytes 3145728 | tf_op jit(solution)/shard_map/second_2/pallas_call | solution.py:231
  52.1 0.8 %copy-done.7 = f32[1024,128]{1,0:T(8,128)} copy-done((f32[1024,128]{1,0:T(8,128)}, f32[1024,128]{1,0:T(8,128)S(1)}, u32[]{:S(2)}) %copy-start.7) | copy-done | bytes 524312
  52.9 0.8 %copy-done.9 = f32[1024,128]{1,0:T(8,128)} copy-done((f32[1024,128]{1,0:T(8,128)}, f32[1024,128]{1,0:T(8,128)S(1)}, u32[]{:S(2)}) %copy-start.9) | copy-done | bytes 524312
  53.7 0.1 reshape.9
  53.7 0.1 reduce_sum.9
  54.0 1.8 %collective-permute-start.14 = (f32[8]{0:T(128)S(1)}, f32[8]{0:T(128)S(1)}, u32[]{:S(2)}, u32[]{:S(2)}) collective-permute-start(f32[8]{0:T(128)S(1)} %reduce_sum.9), channel_id=1, source_target_pairs={{0,3},{1,2},{2,1},{3,0},{4,7},{5,6},{6,5},{7,4},{8,11},{9,10},{10,... | collective-permute-start | bytes 104 | tf_op jit(solution)/shard_map/ppermute | solution.py:292
  55.8 1.0 %copy-done.6 = f32[1024,128]{1,0:T(8,128)S(1)} copy-done((f32[1024,128]{1,0:T(8,128)S(1)}, f32[1024,128]{1,0:T(8,128)}, u32[]{:S(2)}) %copy-start.6) | copy-done | bytes 524312
  56.8 1.0 %copy-done.8 = f32[1024,128]{1,0:T(8,128)S(1)} copy-done((f32[1024,128]{1,0:T(8,128)S(1)}, f32[1024,128]{1,0:T(8,128)}, u32[]{:S(2)}) %copy-start.8) | copy-done | bytes 524312
  57.9 1.0 %copy-done.10 = f32[1024,128]{1,0:T(8,128)S(1)} copy-done((f32[1024,128]{1,0:T(8,128)S(1)}, f32[1024,128]{1,0:T(8,128)}, u32[]{:S(2)}) %copy-start.10) | copy-done | bytes 524312
  58.9 3.1 %finish.1 = (f32[1024,384]{1,0:T(8,128)}, f32[1024,384]{1,0:T(8,128)}) custom-call(f32[1024,128]{1,0:T(8,128)S(1)} %get-tuple-element.35.refs_0_, f32[1024,128]{1,0:T(8,128)S(1)} %get-tuple-element.39.refs_1_, f32[1024,128]{1,0:T(8,128)S(1)} %get-tuple-element.43.refs_2_, f32[1024,128]{1,0:T(8,128)S(1)} %get-tuple-element.44.refs_3_, ...), custom_call_target="tpu_custom_call" | custom-call | flops 603979776 | bytes 4718592 | tf_op jit(solution)/shard_map/finish/pallas_call | solution.py:273
  62.2 4.1 %collective-permute-start.16 = (f32[8]{0:T(128)S(1)}, f32[8]{0:T(128)S(1)}, u32[]{:S(2)}, u32[]{:S(2)}) collective-permute-start(f32[8]{0:T(128)S(1)} %add_add_fusion), channel_id=1, source_target_pairs={{0,8},{1,9},{2,10},{3,11},{4,12},{5,13},{6,14},{7,15},{8,0},{9,1},... | collective-permute-start | bytes 104 | tf_op jit(solution)/shard_map/ppermute | solution.py:292
  66.3 0.3 collective-permute-start.17
  66.5 1.2 %collective-permute-done.16 = f32[8]{0:T(128)S(1)} collective-permute-done((f32[8]{0:T(128)S(1)}, f32[8]{0:T(128)S(1)}, u32[]{:S(2)}, u32[]{:S(2)}) %collective-permute-start.16) | collective-permute-done | bytes 64 | tf_op jit(solution)/shard_map/ppermute | solution.py:292
  67.8 3.8 %collective-permute-done.17 = f32[8]{0:T(128)S(1)} collective-permute-done((f32[8]{0:T(128)S(1)}, f32[8]{0:T(128)S(1)}, u32[]{:S(2)}, u32[]{:S(2)}) %collective-permute-start.17) | collective-permute-done | bytes 64 | tf_op jit(solution)/shard_map/ppermute | solution.py:292
  71.6 0.5 add_multiply_fusion
  (48 shorter events, 0.7 us)
Async XLA Ops:
  0.6 1.4 %copy-start = (f32[1024,384]{1,0:T(8,128)S(1)}, f32[1024,384]{1,0:T(8,128)}, u32[]{:S(2)}) copy-start(f32[1024,384]{1,0:T(8,128)} %refs_7_.3) | copy-start | bytes 4718596
  2.0 5.7 %copy-start.2 = (f32[1024,384]{1,0:T(8,128)S(1)}, f32[1024,384]{1,0:T(8,128)}, u32[]{:S(2)}) copy-start(f32[1024,384]{1,0:T(8,128)} %y_ref.1) | copy-start | bytes 4718596
  2.0 5.7 %copy-start.11 = (bf16[384,48]{1,0:T(8,128)(2,1)S(1)}, bf16[384,48]{1,0:T(8,128)(2,1)}, u32[]{:S(2)}) copy-start(bf16[384,48]{1,0:T(8,128)(2,1)} %constant.10.clone.spread_ref) | copy-start | bytes 110596
  2.0 5.7 %copy-start.12 = (bf16[48,48]{1,0:T(8,128)(2,1)S(1)}, bf16[48,48]{1,0:T(8,128)(2,1)}, u32[]{:S(2)}) copy-start(bf16[48,48]{1,0:T(8,128)(2,1)} %coupling_ref.1) | copy-start | bytes 13828
  2.0 13.2 %copy-start.13 = (s32[96]{0:T(128)S(1)}, s32[96]{0:T(128)}, u32[]{:S(2)}) copy-start(s32[96]{0:T(128)} %rows_ref.11) | copy-start | bytes 1156
  2.1 13.2 %copy-start.14 = (s32[96]{0:T(128)S(1)}, s32[96]{0:T(128)}, u32[]{:S(2)}) copy-start(s32[96]{0:T(128)} %cols_ref.11) | copy-start | bytes 1156
  2.1 13.1 %copy-start.1 = (bf16[96,128,128]{2,1,0:T(8,128)(2,1)S(1)}, bf16[96,128,128]{2,1,0:T(8,128)(2,1)}, u32[]{:S(2)}) copy-start(bf16[96,128,128]{2,1,0:T(8,128)(2,1)} %tiles_ref.11) | copy-start | bytes 9437188
  2.2 13.1 %collective-permute-start.2 = (bf16[1024,128]{1,0:T(8,128)(2,1)S(1)}, bf16[1024,128]{1,0:T(8,128)(2,1)S(1)}, u32[]{:S(2)}, u32[]{:S(2)}) collective-permute-start(bf16[1024,128]{1,0:T(8,128)(2,1)S(1)} %round_first.1.refs_1_), channel_id=1, source_target_pairs={{0,1},{1,2},{2,3},{3,4},{4,5},{5,6},{6,7},{7,8},{8,9},{9,10},{10,1... | collective-permute-start | bytes 786440 | tf_op jit(solution)/shard_map/ppermute | solution.py:314
  2.7 12.6 %collective-permute-start.3 = (bf16[1024,128]{1,0:T(8,128)(2,1)S(1)}, bf16[1024,128]{1,0:T(8,128)(2,1)S(1)}, u32[]{:S(2)}, u32[]{:S(2)}) collective-permute-start(bf16[1024,128]{1,0:T(8,128)(2,1)S(1)} %round_first.1.refs_1_), channel_id=1, source_target_pairs={{1,0},{2,1},{3,2},{4,3},{5,4},{6,5},{7,6},{8,7},{9,8},{10,9},{11,1... | collective-permute-start | bytes 786440 | tf_op jit(solution)/shard_map/ppermute | solution.py:316
  7.7 1.0 %copy-start.3 = (bf16[384,384]{1,0:T(8,128)(2,1)S(1)}, bf16[384,384]{1,0:T(8,128)(2,1)}, u32[]{:S(2)}) copy-start(bf16[384,384]{1,0:T(8,128)(2,1)} %constant.9.clone.same_ref.refs_9_) | copy-start | bytes 884740
  10.1 12.3 %collective-permute-start = (bf16[1024,128]{1,0:T(8,128)(2,1)S(1)}, bf16[1024,128]{1,0:T(8,128)(2,1)S(1)}, u32[]{:S(2)}, u32[]{:S(2)}) collective-permute-start(bf16[1024,128]{1,0:T(8,128)(2,1)S(1)} %get-tuple-element.31.refs_1_), channel_id=1, source_target_pairs={{0,1},{1,2},{2,3},{3,4},{4,5},{5,6},{6,7},{7,8},{8,9},{9,10},{10,1... | collective-permute-start | bytes 786440 | tf_op jit(solution)/shard_map/ppermute | solution.py:314
  10.2 12.3 %collective-permute-start.1 = (bf16[1024,128]{1,0:T(8,128)(2,1)S(1)}, bf16[1024,128]{1,0:T(8,128)(2,1)S(1)}, u32[]{:S(2)}, u32[]{:S(2)}) collective-permute-start(bf16[1024,128]{1,0:T(8,128)(2,1)S(1)} %get-tuple-element.31.refs_1_), channel_id=1, source_target_pairs={{1,0},{2,1},{3,2},{4,3},{5,4},{6,5},{7,6},{8,7},{9,8},{10,9},{11,1... | collective-permute-start | bytes 786440 | tf_op jit(solution)/shard_map/ppermute | solution.py:316
  17.9 11.9 %collective-permute-start.4 = (bf16[1024,128]{1,0:T(8,128)(2,1)S(1)}, bf16[1024,128]{1,0:T(8,128)(2,1)S(1)}, u32[]{:S(2)}, u32[]{:S(2)}) collective-permute-start(bf16[1024,128]{1,0:T(8,128)(2,1)S(1)} %get-tuple-element.36.refs_1_), channel_id=1, source_target_pairs={{0,1},{1,2},{2,3},{3,4},{4,5},{5,6},{6,7},{7,8},{8,9},{9,10},{10,1... | collective-permute-start | bytes 786440 | tf_op jit(solution)/shard_map/ppermute | solution.py:314
  18.0 11.8 %collective-permute-start.5 = (bf16[1024,128]{1,0:T(8,128)(2,1)S(1)}, bf16[1024,128]{1,0:T(8,128)(2,1)S(1)}, u32[]{:S(2)}, u32[]{:S(2)}) collective-permute-start(bf16[1024,128]{1,0:T(8,128)(2,1)S(1)} %get-tuple-element.36.refs_1_), channel_id=1, source_target_pairs={{1,0},{2,1},{3,2},{4,3},{5,4},{6,5},{7,6},{8,7},{9,8},{10,9},{11,1... | collective-permute-start | bytes 786440 | tf_op jit(solution)/shard_map/ppermute | solution.py:316
  25.3 12.0 %collective-permute-start.6 = (bf16[1024,128]{1,0:T(8,128)(2,1)S(1)}, bf16[1024,128]{1,0:T(8,128)(2,1)S(1)}, u32[]{:S(2)}, u32[]{:S(2)}) collective-permute-start(bf16[1024,128]{1,0:T(8,128)(2,1)S(1)} %get-tuple-element.40.refs_1_.refs_5_), channel_id=1, source_target_pairs={{0,1},{1,2},{2,3},{3,4},{4,5},{5,6},{6,7},{7,8},{8,9},{9,10},{10,1... | collective-permute-start | bytes 786440 | tf_op jit(solution)/shard_map/ppermute | solution.py:314
  25.4 11.9 %collective-permute-start.7 = (bf16[1024,128]{1,0:T(8,128)(2,1)S(1)}, bf16[1024,128]{1,0:T(8,128)(2,1)S(1)}, u32[]{:S(2)}, u32[]{:S(2)}) collective-permute-start(bf16[1024,128]{1,0:T(8,128)(2,1)S(1)} %get-tuple-element.40.refs_1_.refs_5_), channel_id=1, source_target_pairs={{1,0},{2,1},{3,2},{4,3},{5,4},{6,5},{7,6},{8,7},{9,8},{10,9},{11,1... | collective-permute-start | bytes 786440 | tf_op jit(solution)/shard_map/ppermute | solution.py:316
  32.8 11.9 %collective-permute-start.8 = (bf16[1024,128]{1,0:T(8,128)(2,1)S(1)}, bf16[1024,128]{1,0:T(8,128)(2,1)S(1)}, u32[]{:S(2)}, u32[]{:S(2)}) collective-permute-start(bf16[1024,128]{1,0:T(8,128)(2,1)S(1)} %get-tuple-element.47.refs_1_.refs_6_), channel_id=1, source_target_pairs={{0,1},{1,2},{2,3},{3,4},{4,5},{5,6},{6,7},{7,8},{8,9},{9,10},{10,1... | collective-permute-start | bytes 786440 | tf_op jit(solution)/shard_map/ppermute | solution.py:314
  32.8 11.8 %collective-permute-start.9 = (bf16[1024,128]{1,0:T(8,128)(2,1)S(1)}, bf16[1024,128]{1,0:T(8,128)(2,1)S(1)}, u32[]{:S(2)}, u32[]{:S(2)}) collective-permute-start(bf16[1024,128]{1,0:T(8,128)(2,1)S(1)} %get-tuple-element.47.refs_1_.refs_6_), channel_id=1, source_target_pairs={{1,0},{2,1},{3,2},{4,3},{5,4},{6,5},{7,6},{8,7},{9,8},{10,9},{11,1... | collective-permute-start | bytes 786440 | tf_op jit(solution)/shard_map/ppermute | solution.py:316
  40.1 8.5 %collective-permute-start.10 = (bf16[1024,128]{1,0:T(8,128)(2,1)S(1)}, bf16[1024,128]{1,0:T(8,128)(2,1)S(1)}, u32[]{:S(2)}, u32[]{:S(2)}) collective-permute-start(bf16[1024,128]{1,0:T(8,128)(2,1)S(1)} %get-tuple-element.50.refs_1_), channel_id=1, source_target_pairs={{0,1},{1,2},{2,3},{3,4},{4,5},{5,6},{6,7},{7,8},{8,9},{9,10},{10,1... | collective-permute-start | bytes 786440 | tf_op jit(solution)/shard_map/ppermute | solution.py:314
  40.2 8.5 %collective-permute-start.11 = (bf16[1024,128]{1,0:T(8,128)(2,1)S(1)}, bf16[1024,128]{1,0:T(8,128)(2,1)S(1)}, u32[]{:S(2)}, u32[]{:S(2)}) collective-permute-start(bf16[1024,128]{1,0:T(8,128)(2,1)S(1)} %get-tuple-element.50.refs_1_), channel_id=1, source_target_pairs={{1,0},{2,1},{3,2},{4,3},{5,4},{6,5},{7,6},{8,7},{9,8},{10,9},{11,1... | collective-permute-start | bytes 786440 | tf_op jit(solution)/shard_map/ppermute | solution.py:316
  47.6 0.8 %copy-start.5 = (f32[1024,128]{1,0:T(8,128)}, f32[1024,128]{1,0:T(8,128)S(1)}, u32[]{:S(2)}) copy-start(f32[1024,128]{1,0:T(8,128)S(1)} %get-tuple-element.49.refs_6_) | copy-start | bytes 1572868
  48.7 7.1 %copy-start.4 = (bf16[384,384]{1,0:T(8,128)(2,1)S(1)}, bf16[384,384]{1,0:T(8,128)(2,1)}, u32[]{:S(2)}) copy-start(bf16[384,384]{1,0:T(8,128)(2,1)} %constant.9.clone.same_ref.refs_9_) | copy-start | bytes 884740
  52.1 0.8 %copy-start.7 = (f32[1024,128]{1,0:T(8,128)}, f32[1024,128]{1,0:T(8,128)S(1)}, u32[]{:S(2)}) copy-start(f32[1024,128]{1,0:T(8,128)S(1)} %get-tuple-element.52.refs_7_) | copy-start | bytes 1572868
  53.9 8.2 %collective-permute-start.12 = (f32[8]{0:T(128)S(1)}, f32[8]{0:T(128)S(1)}, u32[]{:S(2)}, u32[]{:S(2)}) collective-permute-start(f32[8]{0:T(128)S(1)} %reduce_sum.9), channel_id=1, source_target_pairs={{0,1},{1,0},{2,3},{3,2},{4,5},{5,4},{6,7},{7,6},{8,9},{9,8},{10,11... | collective-permute-start | bytes 104 | tf_op jit(solution)/shard_map/ppermute | solution.py:292
  53.9 8.1 %collective-permute-start.13 = (f32[8]{0:T(128)S(1)}, f32[8]{0:T(128)S(1)}, u32[]{:S(2)}, u32[]{:S(2)}) collective-permute-start(f32[8]{0:T(128)S(1)} %reduce_sum.9), channel_id=1, source_target_pairs={{0,2},{1,3},{2,0},{3,1},{4,6},{5,7},{6,4},{7,5},{8,10},{9,11},{10,... | collective-permute-start | bytes 104 | tf_op jit(solution)/shard_map/ppermute | solution.py:292
  54.0 8.1 %collective-permute-start.14 = (f32[8]{0:T(128)S(1)}, f32[8]{0:T(128)S(1)}, u32[]{:S(2)}, u32[]{:S(2)}) collective-permute-start(f32[8]{0:T(128)S(1)} %reduce_sum.9), channel_id=1, source_target_pairs={{0,3},{1,2},{2,1},{3,0},{4,7},{5,6},{6,5},{7,4},{8,11},{9,10},{10,... | collective-permute-start | bytes 104 | tf_op jit(solution)/shard_map/ppermute | solution.py:292
  55.8 1.0 %copy-start.6 = (f32[1024,128]{1,0:T(8,128)S(1)}, f32[1024,128]{1,0:T(8,128)}, u32[]{:S(2)}) copy-start(f32[1024,128]{1,0:T(8,128)} %copy-done.5) | copy-start | bytes 1572868
  56.8 1.0 %copy-start.8 = (f32[1024,128]{1,0:T(8,128)S(1)}, f32[1024,128]{1,0:T(8,128)}, u32[]{:S(2)}) copy-start(f32[1024,128]{1,0:T(8,128)} %copy-done.7) | copy-start | bytes 1572868
  57.9 1.0 %copy-start.10 = (f32[1024,128]{1,0:T(8,128)S(1)}, f32[1024,128]{1,0:T(8,128)}, u32[]{:S(2)}) copy-start(f32[1024,128]{1,0:T(8,128)} %copy-done.9) | copy-start | bytes 1572868
  62.1 4.5 %collective-permute-start.15 = (f32[8]{0:T(128)S(1)}, f32[8]{0:T(128)S(1)}, u32[]{:S(2)}, u32[]{:S(2)}) collective-permute-start(f32[8]{0:T(128)S(1)} %add_add_fusion), channel_id=1, source_target_pairs={{0,4},{1,5},{2,6},{3,7},{4,0},{5,1},{6,2},{7,3},{8,12},{9,13},{10,... | collective-permute-start | bytes 104 | tf_op jit(solution)/shard_map/ppermute | solution.py:292
  62.2 5.6 %collective-permute-start.16 = (f32[8]{0:T(128)S(1)}, f32[8]{0:T(128)S(1)}, u32[]{:S(2)}, u32[]{:S(2)}) collective-permute-start(f32[8]{0:T(128)S(1)} %add_add_fusion), channel_id=1, source_target_pairs={{0,8},{1,9},{2,10},{3,11},{4,12},{5,13},{6,14},{7,15},{8,0},{9,1},... | collective-permute-start | bytes 104 | tf_op jit(solution)/shard_map/ppermute | solution.py:292
  66.3 5.3 %collective-permute-start.17 = (f32[8]{0:T(128)S(1)}, f32[8]{0:T(128)S(1)}, u32[]{:S(2)}, u32[]{:S(2)}) collective-permute-start(f32[8]{0:T(128)S(1)} %add_add_fusion), channel_id=1, source_target_pairs={{0,12},{1,13},{2,14},{3,15},{4,8},{5,9},{6,10},{7,11},{8,4},{9,5},... | collective-permute-start | bytes 104 | tf_op jit(solution)/shard_map/ppermute | solution.py:292
  (1 other events, 0.8 us)
